TPU v7x, 128 devices: a whole 4x4x4 slice. The times are simulated.
128 devices in a mesh: seq: 16 (over z, x), mp: 8 (over y, core).
Axes of the slice: x: 4, y: 4, z: 4, core: 2. Of those that a mesh axis runs over, the one named last changes fastest.
Arguments:
- query_raw: bfloat16 [8, 2048, 6144], P('mp', 'seq'), may hold values from -480 to 480
- key_raw: bfloat16 [8, 2048, 6144], P('mp', 'seq'), may hold values from -480 to 480
- value_rows: bfloat16 [8, 2048, 6144], P('mp', 'seq'), may hold values from -12 to 12
- out_grads: bfloat16 [8, 2048, 6144], P('mp', 'seq'), may hold values from -16 to 16
- image_ids: int32 [8, 2048], P('mp', 'seq'), may hold values from 0 to 7, never falling along the last dimension, each value on 1 to 1024 neighbouring positions
- qk_gains: float32 [2, 128], replicated, may hold values from 0.5 to 6
Outputs:
- query_grads: bfloat16 [8, 2048, 6144], P('mp', 'seq')
- key_grads: bfloat16 [8, 2048, 6144], P('mp', 'seq')
- value_grads: bfloat16 [8, 2048, 6144], P('mp', 'seq')
- gain_grads: float32 [2, 128], replicated
Inputs may be any that keep to these rules, and one draw needn't show every extreme that they name: `image_ids`: ids never fall along a row, every id below 8 occurs in every row, and in every row one image spans exactly 1024 patches.
All inputs are finite; a program needn't handle non-finite values.
Results may differ from a plain program's by a relative error of at most 0.004.
The roundings to bfloat16 on the way count: a program that leaves them out, or rounds other values in their place, can miss the bound.
Values may be sent and summed in bfloat16 or wider, within the bound.
A program may use at most 192 MiB of HBM per device.

v0:
```python
import math

import jax
import jax.numpy as jnp
from jax import lax
from jax.sharding import PartitionSpec as P

EPSILON = 1e-06


def norm_forward(source, gain_row):
    as_float = source.astype(jnp.float32)
    centered = as_float - jnp.mean(as_float, axis=-1, keepdims=True)
    inv_std = lax.rsqrt(jnp.mean(centered * centered, axis=-1, keepdims=True) + EPSILON)
    unit_vals = centered * inv_std
    return ((unit_vals * gain_row).astype(jnp.bfloat16), unit_vals, inv_std)


def norm_backward(tangent, unit_vals, inv_std, gain_row):
    scaled_up = tangent * gain_row
    adjusted = (
        scaled_up
        - jnp.mean(scaled_up, axis=-1, keepdims=True)
        - unit_vals * jnp.mean(scaled_up * unit_vals, axis=-1, keepdims=True)
    )
    return (inv_std * adjusted).astype(jnp.bfloat16)


def group_backward(head_query, head_key, head_value, head_grad, row_images, gains_pair):
    length, heads_here, head_width = head_query.shape
    scaling = head_width ** (-0.5)
    tile_rows = math.gcd(length, 512)
    tile_count = length // tile_rows
    query_lead = jnp.transpose(head_query, (1, 0, 2))
    key_lead = jnp.transpose(head_key, (1, 0, 2))
    value_lead = jnp.transpose(head_value, (1, 0, 2))
    grad_lead = jnp.transpose(head_grad, (1, 0, 2))
    query_norm, query_unit, query_inv = norm_forward(query_lead, gains_pair[0])
    key_norm, key_unit, key_inv = norm_forward(key_lead, gains_pair[1])
    tile_images = row_images.reshape(tile_count, tile_rows)
    tile_first = tile_images[:, 0]
    tile_last = tile_images[:, -1]
    tile_live = (tile_first[:, None] <= tile_last[None, :]) & (
        tile_first[None, :] <= tile_last[:, None]
    )
    key_tiles = [key_norm[:, j * tile_rows : (j + 1) * tile_rows] for j in range(tile_count)]
    value_tiles = [value_lead[:, j * tile_rows : (j + 1) * tile_rows] for j in range(tile_count)]
    score_shape = (heads_here, tile_rows, tile_rows)
    lead_shape = (heads_here, tile_rows, head_width)

    def block_view(source, last_width):
        return jnp.moveaxis(source.reshape(heads_here, tile_count, tile_rows, last_width), 1, 0)

    def block_step(carry_pair, block_inputs):
        key_acc, value_acc = carry_pair
        query_rows, grad_rows, image_rows, live_row, unit_rows, inv_rows = block_inputs
        score_list = []
        for j in range(tile_count):
            image_tile = tile_images[j]
            key_tile = key_tiles[j]

            def compute_scores(query_rows=query_rows, key_tile=key_tile, image_tile=image_tile):
                raw_scores = (
                    jnp.einsum(
                        "hqd,hkd->hqk", query_rows, key_tile, preferred_element_type=jnp.float32
                    )
                    * scaling
                )
                same_image = image_rows[:, None] == image_tile[None, :]
                return jnp.where(same_image[None], raw_scores, -jnp.inf)

            def empty_scores():
                return jnp.full(score_shape, -jnp.inf, jnp.float32)

            score_list.append(lax.cond(live_row[j], compute_scores, empty_scores))
        scores = jnp.concatenate(score_list, axis=2)
        row_max = jnp.max(scores, axis=2, keepdims=True)
        exp_scores = jnp.exp(scores - row_max)
        attn_weights = exp_scores / jnp.sum(exp_scores, axis=2, keepdims=True)
        rounded_weights = attn_weights.astype(jnp.bfloat16)
        output_sum = jnp.zeros(lead_shape, jnp.float32)
        wgrad_list = []
        for j in range(tile_count):
            value_block = value_tiles[j]
            weight_tile = rounded_weights[:, :, j * tile_rows : (j + 1) * tile_rows]

            def compute_values(weight_tile=weight_tile, value_block=value_block):
                return (
                    jnp.einsum(
                        "hqk,hkd->hqd", weight_tile, value_block, preferred_element_type=jnp.float32
                    ),
                    jnp.einsum(
                        "hqd,hkd->hqk", grad_rows, value_block, preferred_element_type=jnp.float32
                    ),
                )

            def empty_values():
                return (jnp.zeros(lead_shape, jnp.float32), jnp.zeros(score_shape, jnp.float32))

            part_out, part_wgrad = lax.cond(live_row[j], compute_values, empty_values)
            output_sum = output_sum + part_out
            wgrad_list.append(part_wgrad)
        weight_grads = jnp.concatenate(wgrad_list, axis=2)
        row_delta = jnp.sum(grad_rows.astype(jnp.float32) * output_sum, axis=-1)
        score_grads = (attn_weights * (weight_grads - row_delta[:, :, None])).astype(jnp.bfloat16)
        query_sum = jnp.zeros(lead_shape, jnp.float32)
        key_list = []
        value_list = []
        for j in range(tile_count):
            key_tile = key_tiles[j]
            grad_scores = score_grads[:, :, j * tile_rows : (j + 1) * tile_rows]
            weight_tile = rounded_weights[:, :, j * tile_rows : (j + 1) * tile_rows]

            def compute_grads(key_tile=key_tile, grad_scores=grad_scores, weight_tile=weight_tile):
                return (
                    jnp.einsum(
                        "hqk,hkd->hqd", grad_scores, key_tile, preferred_element_type=jnp.float32
                    ),
                    jnp.einsum(
                        "hqk,hqd->hkd", grad_scores, query_rows, preferred_element_type=jnp.float32
                    ),
                    jnp.einsum(
                        "hqk,hqd->hkd", weight_tile, grad_rows, preferred_element_type=jnp.float32
                    ),
                )

            def empty_grads():
                zero_rows = jnp.zeros(lead_shape, jnp.float32)
                return (zero_rows, zero_rows, zero_rows)

            part_query, part_key, part_value = lax.cond(live_row[j], compute_grads, empty_grads)
            query_sum = query_sum + part_query
            key_list.append(part_key)
            value_list.append(part_value)
        query_tangent = scaling * query_sum
        query_grads = norm_backward(query_tangent, unit_rows, inv_rows, gains_pair[0])
        gain_query = jnp.sum(query_tangent * unit_rows, axis=1)
        key_acc = key_acc + jnp.concatenate(key_list, axis=1)
        value_acc = value_acc + jnp.concatenate(value_list, axis=1)
        return ((key_acc, value_acc), (query_grads, gain_query))

    zero_full = jnp.zeros((heads_here, length, head_width), jnp.float32)
    block_inputs = (
        block_view(query_norm, head_width),
        block_view(grad_lead, head_width),
        tile_images,
        tile_live,
        block_view(query_unit, head_width),
        block_view(query_inv, 1),
    )
    (key_acc, value_acc), (query_blocks, gain_blocks) = lax.scan(
        block_step, (zero_full, zero_full), block_inputs
    )
    key_tangent = scaling * key_acc
    key_grads = norm_backward(key_tangent, key_unit, key_inv, gains_pair[1])
    gain_terms = jnp.stack([jnp.sum(gain_blocks, axis=0), jnp.sum(key_tangent * key_unit, axis=1)])
    query_out = jnp.moveaxis(query_blocks, 0, 1).reshape(heads_here, length, head_width)
    return (
        jnp.transpose(query_out, (1, 0, 2)),
        jnp.transpose(key_grads, (1, 0, 2)),
        jnp.transpose(value_acc.astype(jnp.bfloat16), (1, 0, 2)),
        gain_terms,
    )


def shards(query_raw, key_raw, value_rows, out_grads, image_ids, qk_gains):
    tok_rows = query_raw.shape[1]
    head_width = qk_gains.shape[1]
    heads_all = query_raw.shape[2] // head_width
    seq_count = lax.axis_size("seq")
    per_device = heads_all // seq_count
    row_images = lax.all_gather(image_ids[0], "seq", axis=0, tiled=True)

    def regroup_view(source):
        return source[0].reshape(tok_rows, seq_count, per_device, head_width)

    patch_parts = (
        regroup_view(query_raw),
        regroup_view(key_raw),
        regroup_view(value_rows),
        regroup_view(out_grads),
    )
    arrived_parts = (
        lax.all_to_all(patch_parts[0], "seq", split_axis=1, concat_axis=0, tiled=True),
        lax.all_to_all(patch_parts[1], "seq", split_axis=1, concat_axis=0, tiled=True),
        lax.all_to_all(patch_parts[2], "seq", split_axis=1, concat_axis=0, tiled=True),
        lax.all_to_all(patch_parts[3], "seq", split_axis=1, concat_axis=0, tiled=True),
    )
    group_query, group_key, group_value, group_grad = [piece[:, 0] for piece in arrived_parts]
    query_part, key_part, value_part, term_part = group_backward(
        group_query, group_key, group_value, group_grad, row_images, qk_gains
    )
    query_back = lax.all_to_all(query_part[:, None], "seq", split_axis=0, concat_axis=1, tiled=True)
    key_back = lax.all_to_all(key_part[:, None], "seq", split_axis=0, concat_axis=1, tiled=True)
    value_back = lax.all_to_all(value_part[:, None], "seq", split_axis=0, concat_axis=1, tiled=True)
    term_back = term_part[:, None]
    gain_terms = jnp.sum(term_back[:, 0], axis=1)
    gain_total = lax.psum(gain_terms, ("seq", "mp")) * (tok_rows * seq_count * heads_all) ** (-0.5)

    def merge_heads(source):
        return source.reshape(1, tok_rows, heads_all * head_width)

    return (merge_heads(query_back), merge_heads(key_back), merge_heads(value_back), gain_total)


def solution(mesh):
    placed = (
        P("mp", "seq", None),
        P("mp", "seq", None),
        P("mp", "seq", None),
        P("mp", "seq", None),
        P("mp", "seq"),
        P(),
    )
    return jax.shard_map(
        shards,
        mesh=mesh,
        in_specs=placed,
        out_specs=(P("mp", "seq", None), P("mp", "seq", None), P("mp", "seq", None), P()),
        check_vma=False,
    )
```

profile of v0, /device:TPU:1, one launch (start us, length us, event | category | flops | bytes accessed | tf_op | source)
XLA Modules:
  0.0 911.6 jit_solution(8855479080803968688)
XLA Ops:
  3.3 8.6 all-to-all-start.1
  13.5 30.7 %all-gather = s32[1,2048]{1,0:T(1,128)S(1)} all-gather(s32[1,128]{1,0:T(1,128)S(1)} %copy-done.54), channel_id=2, replica_groups=mesh['seq'=16,'mp'=8] {'seq'}, dimensions={1}, use_global_device_ids=true | all-gather | bytes 8704 | tf_op jit(solution)/shard_map/all_gather | solution.py:172
  45.9 4.4 all-to-all-start
  61.4 7.5 all-to-all-done
  68.9 4.5 all-to-all-start.3
  86.9 4.9 all-to-all-done.3
  91.8 4.4 all-to-all-start.2
  98.9 8.0 multiply_convert_fusion.2
  110.1 4.5 all-to-all-done.2
  117.2 532.4 %while.17 = (s32[]{:T(128)}, f32[3,2048,128]{2,1,0:T(8,128)}, f32[3,2048,128]{2,1,0:T(8,128)}, bf16[4,3,512,128]{3,2,0,1:T(8,128)(2,1)}, f32[4,3,128]{2,1,0:T(4,...) while((s32[]{:T(128)}, f32[3,2048,128]{2,1,0:T(8,128)}, ...), condition=%wide.region_38.39_spmd.clone, body=%wide.region_4.38_spmd.clone.sunk | while | flops 4923714560 | bytes 483076288 | solution.py:151
  150.4 4.3 conditional.39
  169.9 6.0 fusion.93
  199.1 10.2 %fusion.96 = bf16[3,512,2048]{1,2,0:T(8,128)(2,1)} fusion(f32[3,512,512]{1,2,0:T(8,128)} %get-tuple-element.932, f32[3,512,512]{1,2,0:T(8,128)} %copy-done.17, f32[3,512,512]{1,2,0:T(8,128)} %copy-done.19, f32[3,512,512]{1,2,0:T(8,128)} %copy-done.18, f32[3,512]{1,0:T(4,128)S(1)} %multiply_reduce_fusion.8, f32[3,512]{1,0:T(4,128)S(1)} %fusion.93, ...), kind=kLoop, calls=%fused_computation.28.clone.1 | loop fusion | flops 34603008 | bytes 31475712 | tf_op jit(solution)/shard_map/while/body/eval_jaxpr/convert_element_type | solution.py:105
  209.3 15.7 %conditional.47 = (f32[3,512,128]{2,1,0:T(8,128)}, f32[3,512,128]{2,1,0:T(8,128)S(1)}, f32[3,512,128]{2,1,0:T(8,128)}) conditional(s32[]{:T(128)} %bitcast.195, () %tuple.283, (bf16[3,512,2048]{1,2,0:T(8,128)(2,1)}, bf16[3,512,128]{2,1,0:T(8,128)(2,1)}, bf16[3,512,128]{2,1,0:T(8,128)(2,1)S(1)}, bf16[3,512,512]{1,2,0:T(8,128)(2,1)}, ...), branch_computations={%region_27.27_spmd, %region_28.28_spmd} | conditional | flops 603979776 | bytes 28704848 | solution.py:131
  209.3 9.0 copy.212
  226.0 16.2 %conditional.46 = (f32[3,512,128]{2,1,0:T(8,128)}, f32[3,512,128]{2,1,0:T(8,128)}, f32[3,512,128]{2,1,0:T(8,128)}) conditional(s32[]{:T(128)} %bitcast.196, () %tuple.281, (bf16[3,512,2048]{1,2,0:T(8,128)(2,1)}, bf16[3,512,128]{2,1,0:T(8,128)(2,1)S(1)}, bf16[3,512,128]{2,1,0:T(8,128)(2,1)S(1)}, bf16[3,512,512]{1,2,0:T(8,128)(2,1)S(1)}, ...), branch_computations={%region_29.29_spmd, %region_30.30_spmd} | conditional | flops 603979776 | bytes 22413364 | solution.py:131
  226.0 8.9 copy.213
  253.8 6.7 maximum_add_fusion.3
  277.7 4.3 conditional.39
  297.2 6.0 fusion.93
  326.3 10.2 %fusion.96 = bf16[3,512,2048]{1,2,0:T(8,128)(2,1)} fusion(f32[3,512,512]{1,2,0:T(8,128)} %get-tuple-element.932, f32[3,512,512]{1,2,0:T(8,128)} %copy-done.17, f32[3,512,512]{1,2,0:T(8,128)} %copy-done.19, f32[3,512,512]{1,2,0:T(8,128)} %copy-done.18, f32[3,512]{1,0:T(4,128)S(1)} %multiply_reduce_fusion.8, f32[3,512]{1,0:T(4,128)S(1)} %fusion.93, ...), kind=kLoop, calls=%fused_computation.28.clone.1 | loop fusion | flops 34603008 | bytes 31475712 | tf_op jit(solution)/shard_map/while/body/eval_jaxpr/convert_element_type | solution.py:105
  336.6 15.7 %conditional.47 = (f32[3,512,128]{2,1,0:T(8,128)}, f32[3,512,128]{2,1,0:T(8,128)S(1)}, f32[3,512,128]{2,1,0:T(8,128)}) conditional(s32[]{:T(128)} %bitcast.195, () %tuple.283, (bf16[3,512,2048]{1,2,0:T(8,128)(2,1)}, bf16[3,512,128]{2,1,0:T(8,128)(2,1)}, bf16[3,512,128]{2,1,0:T(8,128)(2,1)S(1)}, bf16[3,512,512]{1,2,0:T(8,128)(2,1)}, ...), branch_computations={%region_27.27_spmd, %region_28.28_spmd} | conditional | flops 603979776 | bytes 28704848 | solution.py:131
  336.6 9.0 copy.212
  353.3 16.2 %conditional.46 = (f32[3,512,128]{2,1,0:T(8,128)}, f32[3,512,128]{2,1,0:T(8,128)}, f32[3,512,128]{2,1,0:T(8,128)}) conditional(s32[]{:T(128)} %bitcast.196, () %tuple.281, (bf16[3,512,2048]{1,2,0:T(8,128)(2,1)}, bf16[3,512,128]{2,1,0:T(8,128)(2,1)S(1)}, bf16[3,512,128]{2,1,0:T(8,128)(2,1)S(1)}, bf16[3,512,512]{1,2,0:T(8,128)(2,1)S(1)}, ...), branch_computations={%region_29.29_spmd, %region_30.30_spmd} | conditional | flops 603979776 | bytes 22413364 | solution.py:131
  353.3 8.9 copy.213
  381.0 7.7 maximum_add_fusion.3
  425.4 6.0 fusion.93
  454.7 10.2 %fusion.96 = bf16[3,512,2048]{1,2,0:T(8,128)(2,1)} fusion(f32[3,512,512]{1,2,0:T(8,128)} %get-tuple-element.932, f32[3,512,512]{1,2,0:T(8,128)} %copy-done.17, f32[3,512,512]{1,2,0:T(8,128)} %copy-done.19, f32[3,512,512]{1,2,0:T(8,128)} %copy-done.18, f32[3,512]{1,0:T(4,128)S(1)} %multiply_reduce_fusion.8, f32[3,512]{1,0:T(4,128)S(1)} %fusion.93, ...), kind=kLoop, calls=%fused_computation.28.clone.1 | loop fusion | flops 34603008 | bytes 31475712 | tf_op jit(solution)/shard_map/while/body/eval_jaxpr/convert_element_type | solution.py:105
  470.7 16.9 %conditional.45 = (f32[3,512,128]{2,1,0:T(8,128)}, f32[3,512,128]{2,1,0:T(8,128)S(1)}, f32[3,512,128]{2,1,0:T(8,128)}) conditional(s32[]{:T(128)} %bitcast.194, () %tuple.279, (bf16[3,512,2048]{1,2,0:T(8,128)(2,1)}, bf16[3,512,128]{2,1,0:T(8,128)(2,1)}, bf16[3,512,128]{2,1,0:T(8,128)(2,1)S(1)}, bf16[3,512,512]{1,2,0:T(8,128)(2,1)}, ...), branch_computations={%region_31.31_spmd, %region_32.32_spmd} | conditional | flops 603979776 | bytes 23986256 | solution.py:131
  470.7 9.0 copy.214
  488.5 16.3 %conditional.44 = (f32[3,512,128]{2,1,0:T(8,128)}, f32[3,512,128]{2,1,0:T(8,128)}, f32[3,512,128]{2,1,0:T(8,128)}) conditional(s32[]{:T(128)} %bitcast.192, () %tuple.261, (bf16[3,512,2048]{1,2,0:T(8,128)(2,1)}, bf16[3,512,128]{2,1,0:T(8,128)(2,1)S(1)}, bf16[3,512,128]{2,1,0:T(8,128)(2,1)S(1)}, bf16[3,512,512]{1,2,0:T(8,128)(2,1)S(1)}, ...), branch_computations={%region_33.33_spmd, %region_34.34_spmd} | conditional | flops 603979776 | bytes 22413364 | solution.py:131
  488.5 8.9 copy.215
  510.6 7.7 maximum_add_fusion.3
  555.1 6.0 fusion.93
  584.3 10.2 %fusion.96 = bf16[3,512,2048]{1,2,0:T(8,128)(2,1)} fusion(f32[3,512,512]{1,2,0:T(8,128)} %get-tuple-element.932, f32[3,512,512]{1,2,0:T(8,128)} %copy-done.17, f32[3,512,512]{1,2,0:T(8,128)} %copy-done.19, f32[3,512,512]{1,2,0:T(8,128)} %copy-done.18, f32[3,512]{1,0:T(4,128)S(1)} %multiply_reduce_fusion.8, f32[3,512]{1,0:T(4,128)S(1)} %fusion.93, ...), kind=kLoop, calls=%fused_computation.28.clone.1 | loop fusion | flops 34603008 | bytes 31475712 | tf_op jit(solution)/shard_map/while/body/eval_jaxpr/convert_element_type | solution.py:105
  600.3 16.9 %conditional.45 = (f32[3,512,128]{2,1,0:T(8,128)}, f32[3,512,128]{2,1,0:T(8,128)S(1)}, f32[3,512,128]{2,1,0:T(8,128)}) conditional(s32[]{:T(128)} %bitcast.194, () %tuple.279, (bf16[3,512,2048]{1,2,0:T(8,128)(2,1)}, bf16[3,512,128]{2,1,0:T(8,128)(2,1)}, bf16[3,512,128]{2,1,0:T(8,128)(2,1)S(1)}, bf16[3,512,512]{1,2,0:T(8,128)(2,1)}, ...), branch_computations={%region_31.31_spmd, %region_32.32_spmd} | conditional | flops 603979776 | bytes 23986256 | solution.py:131
  600.3 9.0 copy.214
  618.1 16.3 %conditional.44 = (f32[3,512,128]{2,1,0:T(8,128)}, f32[3,512,128]{2,1,0:T(8,128)}, f32[3,512,128]{2,1,0:T(8,128)}) conditional(s32[]{:T(128)} %bitcast.192, () %tuple.261, (bf16[3,512,2048]{1,2,0:T(8,128)(2,1)}, bf16[3,512,128]{2,1,0:T(8,128)(2,1)S(1)}, bf16[3,512,128]{2,1,0:T(8,128)(2,1)S(1)}, bf16[3,512,512]{1,2,0:T(8,128)(2,1)S(1)}, ...), branch_computations={%region_33.33_spmd, %region_34.34_spmd} | conditional | flops 603979776 | bytes 22413364 | solution.py:131
  618.1 8.9 copy.215
  640.2 7.7 maximum_add_fusion.3
  649.6 6.0 multiply_reduce_fusion.2
  659.6 10.7 %copy.231 = bf16[2048,1,3,128]{3,2,1,0:T(4,128)(2,1)} copy(bf16[2048,1,3,128]{3,0,2,1:T(8,128)(2,1)S(1)} %fusion.28) | data formatting | bytes 3145728 | tf_op jit(solution)/shard_map/broadcast_in_dim | solution.py:194
  670.4 4.6 all-to-all-start.5
  675.3 10.7 %copy.234 = bf16[2048,1,3,128]{3,2,1,0:T(4,128)(2,1)} copy(bf16[2048,1,3,128]{3,0,2,1:T(8,128)(2,1)S(1)} %convert_bitcast_fusion.2) | data formatting | bytes 3145728 | tf_op jit(solution)/shard_map/broadcast_in_dim | solution.py:195
  686.0 8.9 all-to-all-done.5
  702.9 15.6 %all-to-all-done.6 = bf16[2048,1,3,128]{3,2,1,0:T(4,128)(2,1)S(1)} async-done(((bf16[2048,1,3,128]{3,2,1,0:T(4,128)(2,1)}), bf16[2048,1,3,128]{3,2,1,0:T(4,128)(2,1)S(1)}, u32[]{:S(2)}, u32[]{:S(2)}) %all-to-all-start.6) | async-done | bytes 1572896 | tf_op jit(solution)/shard_map/all_to_all | solution.py:195
  718.5 4.4 all-to-all-start.4
  723.0 170.6 %psum.7 = f32[2,128]{1,0:T(2,128)S(1)} all-reduce(f32[2,128]{1,0:T(2,128)S(1)} %maximum_reduce_fusion), channel_id=1, replica_groups=mesh['seq'=16,'mp'=8] {'seq','mp'}, use_global_device_ids=true, to_apply=%region_44.45 | all-reduce | flops 256 | bytes 2048 | tf_op jit(solution)/shard_map/psum | solution.py:198
  (607 shorter events, 484.3 us)
Async XLA Ops:
  0.6 11.3 %copy-start.40 = (bf16[1,128,6144]{2,1,0:T(8,128)(2,1)S(1)}, bf16[1,128,6144]{2,1,0:T(8,128)(2,1)}, u32[]{:S(2)}) copy-start(bf16[1,128,6144]{2,1,0:T(8,128)(2,1)} %param.32) | copy-start | bytes 4718596
  3.3 10.1 %copy-start.54 = (s32[1,128]{1,0:T(1,128)S(1)}, s32[1,128]{1,0:T(1,128)}, u32[]{:S(2)}) copy-start(s32[1,128]{1,0:T(1,128)} %param.36) | copy-start | bytes 1540
  3.3 42.6 %all-to-all-start.1 = ((bf16[128,16,3,128]{0,3,2,1:T(8,128)(2,1)}), bf16[128,16,3,128]{0,3,2,1:T(8,128)(2,1)S(1)}, u32[]{:S(2)}, u32[]{:S(2)}) async-start(bf16[128,16,3,128]{0,3,2,1:T(8,128)(2,1)} %bitcast.13), calls=%async_computation.1 | async-start | bytes 3145728 | tf_op jit(solution)/shard_map/all_to_all | solution.py:185
  13.5 37.8 %copy-start.41 = (bf16[1,128,6144]{2,1,0:T(8,128)(2,1)S(1)}, bf16[1,128,6144]{2,1,0:T(8,128)(2,1)}, u32[]{:S(2)}) copy-start(bf16[1,128,6144]{2,1,0:T(8,128)(2,1)} %param.34) | copy-start | bytes 4718596
  45.9 23.0 %all-to-all-start = ((bf16[128,16,3,128]{0,3,2,1:T(8,128)(2,1)}), bf16[128,16,3,128]{0,3,2,1:T(8,128)(2,1)}, u32[]{:S(2)}, u32[]{:S(2)}) async-start(bf16[128,16,3,128]{0,3,2,1:T(8,128)(2,1)} %bitcast.4), calls=%async_computation | async-start | bytes 3145728 | tf_op jit(solution)/shard_map/all_to_all | solution.py:184
  60.5 38.4 %copy-start.23 = (f32[16,128,1,3,128]{4,1,0,3,2:T(8,128)}, f32[16,128,1,3,128]{4,1,0,3,2:T(8,128)S(1)}, u32[]{:S(2)}) copy-start(f32[16,128,1,3,128]{4,1,0,3,2:T(8,128)S(1)} %copy.219) | copy-start | bytes 9437188
  61.4 37.5 %copy-start.42 = (f32[3,2048]{1,0:T(4,128)}, f32[3,2048]{1,0:T(4,128)S(1)}, u32[]{:S(2)}) copy-start(f32[3,2048]{1,0:T(4,128)S(1)} %broadcast_multiply_fusion.4) | copy-start | bytes 73732
  68.9 22.9 %all-to-all-start.3 = ((bf16[128,16,3,128]{0,3,2,1:T(8,128)(2,1)}), bf16[128,16,3,128]{0,3,2,1:T(8,128)(2,1)}, u32[]{:S(2)}, u32[]{:S(2)}) async-start(bf16[128,16,3,128]{0,3,2,1:T(8,128)(2,1)} %bitcast.208), calls=%async_computation.3 | async-start | bytes 3145728 | tf_op jit(solution)/shard_map/all_to_all | solution.py:186
  86.9 12.0 %copy-start.46 = (f32[3,2048]{1,0:T(4,128)}, f32[3,2048]{1,0:T(4,128)S(1)}, u32[]{:S(2)}) copy-start(f32[3,2048]{1,0:T(4,128)S(1)} %add_rsqrt_fusion) | copy-start | bytes 73732
  91.8 22.8 %all-to-all-start.2 = ((bf16[128,16,3,128]{0,3,2,1:T(8,128)(2,1)}), bf16[128,16,3,128]{0,3,2,1:T(8,128)(2,1)}, u32[]{:S(2)}, u32[]{:S(2)}) async-start(bf16[128,16,3,128]{0,3,2,1:T(8,128)(2,1)} %bitcast.207), calls=%async_computation.2 | async-start | bytes 3145728 | tf_op jit(solution)/shard_map/all_to_all | solution.py:187
  169.9 6.0 copy-start
  169.9 6.0 copy-start.2
  169.9 6.6 copy-start.3
  209.3 15.7 %copy-start.13 = (bf16[3,512,512]{1,2,0:T(8,128)(2,1)S(1)}, bf16[3,512,512]{1,2,0:T(8,128)(2,1)}, u32[]{:S(2)}) copy-start(bf16[3,512,512]{1,2,0:T(8,128)(2,1)} %get-tuple-element.935) | copy-start | bytes 4718596 | tf_op jit(solution)/shard_map/while
  209.3 15.7 %copy-start.38 = (bf16[3,512,128]{2,1,0:T(8,128)(2,1)S(1)}, bf16[3,512,128]{2,1,0:T(8,128)(2,1)}, u32[]{:S(2)}) copy-start(bf16[3,512,128]{2,1,0:T(8,128)(2,1)} %get-tuple-element.1058) | copy-start | bytes 1179652 | tf_op jit(solution)/shard_map/while
  253.8 8.3 copy-start.56
  297.2 6.0 copy-start
  297.2 6.0 copy-start.2
  297.2 6.6 copy-start.3
  336.6 15.7 %copy-start.13 = (bf16[3,512,512]{1,2,0:T(8,128)(2,1)S(1)}, bf16[3,512,512]{1,2,0:T(8,128)(2,1)}, u32[]{:S(2)}) copy-start(bf16[3,512,512]{1,2,0:T(8,128)(2,1)} %get-tuple-element.935) | copy-start | bytes 4718596 | tf_op jit(solution)/shard_map/while
  336.6 15.7 %copy-start.38 = (bf16[3,512,128]{2,1,0:T(8,128)(2,1)S(1)}, bf16[3,512,128]{2,1,0:T(8,128)(2,1)}, u32[]{:S(2)}) copy-start(bf16[3,512,128]{2,1,0:T(8,128)(2,1)} %get-tuple-element.1058) | copy-start | bytes 1179652 | tf_op jit(solution)/shard_map/while
  381.0 9.4 %copy-start.56 = (pred[4,4]{1,0:T(4,128)(4,1)S(1)}, pred[4,4]{1,0:T(4,128)(4,1)}, u32[]{:S(2)}) copy-start(pred[4,4]{1,0:T(4,128)(4,1)} %copy-done.55) | copy-start | bytes 52 | tf_op jit(solution)/shard_map/while
  425.4 6.0 copy-start
  425.4 6.0 copy-start.2
  425.4 6.6 copy-start.3
  470.7 16.9 %copy-start.11 = (bf16[3,512,512]{1,2,0:T(8,128)(2,1)S(1)}, bf16[3,512,512]{1,2,0:T(8,128)(2,1)}, u32[]{:S(2)}) copy-start(bf16[3,512,512]{1,2,0:T(8,128)(2,1)} %get-tuple-element.931) | copy-start | bytes 4718596 | tf_op jit(solution)/shard_map/while
  470.7 16.9 %copy-start.36 = (bf16[3,512,128]{2,1,0:T(8,128)(2,1)S(1)}, bf16[3,512,128]{2,1,0:T(8,128)(2,1)}, u32[]{:S(2)}) copy-start(bf16[3,512,128]{2,1,0:T(8,128)(2,1)} %get-tuple-element.1060) | copy-start | bytes 1179652 | tf_op jit(solution)/shard_map/while
  470.7 9.0 copy-start.37
  487.6 17.2 %copy-start.53 = (f32[2,128]{1,0:T(2,128)S(1)}, f32[2,128]{1,0:T(2,128)}, u32[]{:S(2)}) copy-start(f32[2,128]{1,0:T(2,128)} %get-tuple-element.1067) | copy-start | bytes 3076 | tf_op jit(solution)/shard_map/while
  510.6 9.4 %copy-start.56 = (pred[4,4]{1,0:T(4,128)(4,1)S(1)}, pred[4,4]{1,0:T(4,128)(4,1)}, u32[]{:S(2)}) copy-start(pred[4,4]{1,0:T(4,128)(4,1)} %copy-done.55) | copy-start | bytes 52 | tf_op jit(solution)/shard_map/while
  555.1 6.0 copy-start
  555.1 6.0 copy-start.2
  555.1 6.6 copy-start.3
  600.3 16.9 %copy-start.11 = (bf16[3,512,512]{1,2,0:T(8,128)(2,1)S(1)}, bf16[3,512,512]{1,2,0:T(8,128)(2,1)}, u32[]{:S(2)}) copy-start(bf16[3,512,512]{1,2,0:T(8,128)(2,1)} %get-tuple-element.931) | copy-start | bytes 4718596 | tf_op jit(solution)/shard_map/while
  600.3 16.9 %copy-start.36 = (bf16[3,512,128]{2,1,0:T(8,128)(2,1)S(1)}, bf16[3,512,128]{2,1,0:T(8,128)(2,1)}, u32[]{:S(2)}) copy-start(bf16[3,512,128]{2,1,0:T(8,128)(2,1)} %get-tuple-element.1060) | copy-start | bytes 1179652 | tf_op jit(solution)/shard_map/while
  600.3 9.0 copy-start.37
  617.2 17.2 %copy-start.53 = (f32[2,128]{1,0:T(2,128)S(1)}, f32[2,128]{1,0:T(2,128)}, u32[]{:S(2)}) copy-start(f32[2,128]{1,0:T(2,128)} %get-tuple-element.1067) | copy-start | bytes 3076 | tf_op jit(solution)/shard_map/while
  640.2 9.4 %copy-start.56 = (pred[4,4]{1,0:T(4,128)(4,1)S(1)}, pred[4,4]{1,0:T(4,128)(4,1)}, u32[]{:S(2)}) copy-start(pred[4,4]{1,0:T(4,128)(4,1)} %copy-done.55) | copy-start | bytes 52 | tf_op jit(solution)/shard_map/while
  649.6 6.1 copy-start.22
  649.6 6.1 copy-start.24
  649.6 6.1 copy-start.43
  649.6 6.1 copy-start.47
  649.6 6.1 copy-start.51
  659.6 15.4 %copy-start.25 = (f32[3,2048,128]{2,1,0:T(8,128)S(1)}, f32[3,2048,128]{2,1,0:T(8,128)}, u32[]{:S(2)}) copy-start(f32[3,2048,128]{2,1,0:T(8,128)} %get-tuple-element.295) | copy-start | bytes 9437188
  670.4 24.5 %all-to-all-start.5 = ((bf16[2048,1,3,128]{3,2,1,0:T(4,128)(2,1)}), bf16[2048,1,3,128]{3,2,1,0:T(4,128)(2,1)}, u32[]{:S(2)}, u32[]{:S(2)}) async-start(bf16[2048,1,3,128]{3,2,1,0:T(4,128)(2,1)} %copy.231), calls=%async_computation.5 | async-start | bytes 4194304 | tf_op jit(solution)/shard_map/all_to_all | solution.py:194
  694.9 23.5 %all-to-all-start.6 = ((bf16[2048,1,3,128]{3,2,1,0:T(4,128)(2,1)}), bf16[2048,1,3,128]{3,2,1,0:T(4,128)(2,1)S(1)}, u32[]{:S(2)}, u32[]{:S(2)}) async-start(bf16[2048,1,3,128]{3,2,1,0:T(4,128)(2,1)} %copy.234), calls=%async_computation.6 | async-start | bytes 4194304 | tf_op jit(solution)/shard_map/all_to_all | solution.py:195
  698.7 24.2 %copy-start.50 = (f32[4,3,128]{2,1,0:T(4,128)S(1)}, f32[4,3,128]{2,1,0:T(4,128)}, u32[]{:S(2)}) copy-start(f32[4,3,128]{2,1,0:T(4,128)} %get-tuple-element.296) | copy-start | bytes 18436
  718.5 188.6 %all-to-all-start.4 = ((bf16[2048,1,3,128]{3,2,1,0:T(4,128)(2,1)}), bf16[2048,1,3,128]{3,2,1,0:T(4,128)(2,1)}, u32[]{:S(2)}, u32[]{:S(2)}) async-start(bf16[2048,1,3,128]{3,2,1,0:T(4,128)(2,1)} %copy.228), calls=%async_computation.4 | async-start | bytes 4194304 | tf_op jit(solution)/shard_map/all_to_all | solution.py:193
  (115 other events, 276.9 us)
where the time goes:
time: 924 us; the launch traced here: 912 us
  local copies, waits for them, and re-layouts  309 us (33%)
  blocking collectives  201 us (22%)
  other arithmetic  192 us (21%)
  matrix products  102 us (11%)
  waiting for transfers between devices  41.5 us (4%)
  starting transfers between devices  34.6 us (4%)
  loops' own time  29.7 us (3%)
    psum x1, blocking collectives, shards(): lax.psum(gain_terms, ('seq', 'mp'))  171 us
    another operation x56, local copies, waits for them, and re-layouts  107 us
    cond x16, local copies, waits for them, and re-layouts, block_step(): score_list.append(lax.cond(live_row[j], compute_scores, empty_scores))  52.1 us
    while x232, local copies, waits for them, and re-layouts  49.1 us
    convert_element_type x4, other arithmetic, block_step(): (attn_weights * (weight_grads - row_delta[:, :, None])).astype(jnp.bfloat16)  41 us
    all_gather x1, blocking collectives, shards(): row_images = lax.all_gather(image_ids[0], 'seq', axis=0, tiled=True)  30.7 us
    add x4, other arithmetic, block_step(): key_acc = key_acc + jnp.concatenate(key_list, axis=1)  29.7 us
    another operation x1, loops' own time, group_backward(): lax.scan(block_step, (zero_full, zero_full), block_inputs)  29 us
  transfers between devices with their start and end apart: 7, of which 5 were waited for; matrix products, arithmetic and copies ran while one was open for 8% of the time, Pallas kernels for 0%

commit v1 on v0

v1 whole, which is shorter than its diff:
```python
import functools
import math

import jax
import jax.numpy as jnp
from jax import lax
from jax.experimental import pallas as pl
from jax.experimental.pallas import tpu as pltpu
from jax.sharding import PartitionSpec as P

MESH = pl.DeviceIdType.MESH
EPSILON = 1e-06
BAN = -32768.0
CLASSES = 8
QT = 256
KT = 512
RT = 256
MOST = 1024
F32 = jnp.float32
BF16 = jnp.bfloat16


def contract_last(a, b):
    return lax.dot_general(a, b, (((1,), (1,)), ((), ())), preferred_element_type=F32)


def matmul(a, b):
    return lax.dot_general(a, b, (((1,), (0,)), ((), ())), preferred_element_type=F32)


def fold(x):
    return x.reshape(x.shape[0] // 8, 8, x.shape[1])


def kernel(
    n, m, heads, tok, hd,
    q_hbm, k_hbm, v_hbm, g_hbm, ids_ref, gains_ref,
    oq_hbm, ok_hbm, ov_hbm, gain_ref,
    in_buf, out_buf, id_src, id_buf, q_aug, k_aug, k_turned, unit_buf, inv_buf,
    s_buf, w_buf, p_buf, dk_acc, dv_acc, gain_acc, gain_seq, gain_mp,
    in_send, in_recv, id_send, id_recv, out_send, out_recv, gain_send, gain_recv,
):
    seq, mp = lax.axis_index("seq"), lax.axis_index("mp")
    length = n * tok
    side = math.isqrt(n)
    scaling = hd ** (-0.5)
    exponent = scaling * math.log2(math.e)

    def partner(i):
        z = lax.rem(seq // side + i // side, side)
        x = lax.rem(lax.rem(seq, side) + lax.rem(i, side), side)
        return z * side + x

    def mp_partner(i):
        return lax.rem(mp + i, m)

    def remote(src, dst, send, recv, to_seq, to_mp):
        return pltpu.make_async_remote_copy(
            src_ref=src, dst_ref=dst, send_sem=send, recv_sem=recv,
            device_id=(to_seq, to_mp), device_id_type=MESH,
        )

    barrier = pltpu.get_barrier_semaphore()

    def greet_seq(i, c):
        pl.semaphore_signal(barrier, inc=1, device_id=(partner(i), mp), device_id_type=MESH)
        return c

    def greet_mp(i, c):
        pl.semaphore_signal(barrier, inc=1, device_id=(seq, mp_partner(i)), device_id_type=MESH)
        return c

    lax.fori_loop(1, n, greet_seq, 0)
    lax.fori_loop(1, m, greet_mp, 0)
    id_src[...] = jnp.broadcast_to(ids_ref[...], (8, tok))
    id_buf[pl.ds(pl.multiple_of(seq * 8, 8), 8), :] = jnp.broadcast_to(ids_ref[...], (8, tok))
    pl.semaphore_wait(barrier, n - 1 + m - 1)

    def send_ids(i, c):
        remote(
            id_src, id_buf.at[pl.ds(pl.multiple_of(seq * 8, 8), 8)],
            id_send.at[0], id_recv.at[0], partner(i), mp,
        ).start()
        return c

    lax.fori_loop(1, n, send_ids, 0)
    sources = (q_hbm, k_hbm, v_hbm, g_hbm)

    def in_rows(h, a, s):
        return pl.ds(pl.multiple_of(((h * 4 + a) * n + s) * tok, tok), tok)

    def lanes(owner, h):
        return pl.ds(pl.multiple_of((owner * heads + h) * hd, hd), hd)

    def send_head(h, c):
        for a in range(4):
            pltpu.make_async_copy(
                sources[a].at[0, :, lanes(seq, h)], in_buf.at[in_rows(h, a, seq)], in_recv.at[h]
            ).start()

            def send_one(i, c, a=a):
                to = partner(i)
                remote(
                    sources[a].at[0, :, lanes(to, h)], in_buf.at[in_rows(h, a, seq)],
                    in_send.at[0], in_recv.at[h], to, mp,
                ).start()
                return c

            lax.fori_loop(1, n, send_one, 0)
        return c

    lax.fori_loop(0, heads, send_head, 0)

    ids_got = id_buf.at[pl.ds(0, (n - 1) * 8)]
    pltpu.make_async_copy(ids_got, ids_got, id_recv.at[0]).wait()
    lane = lax.broadcasted_iota(jnp.int32, (tok, hd), 1)

    def features(s, c):
        row = id_buf[pl.ds(pl.multiple_of(s * 8, 8), 8), :].astype(F32)[:1]
        image = jnp.transpose(jnp.broadcast_to(row, (hd, tok))).astype(jnp.int32)
        same = image == lane
        rows = pl.ds(pl.multiple_of(s * tok, tok), tok)
        q_aug[rows, hd:] = jnp.where(same, 1.0, 0.0).astype(BF16)
        k_aug[rows, hd:] = jnp.where(jnp.logical_and(lane < CLASSES, ~same), BAN, 0.0).astype(BF16)
        return c

    lax.fori_loop(0, n, features, 0)
    gain_acc[...] = jnp.zeros_like(gain_acc)

    def mean(x):
        return jnp.sum(x, axis=-1, keepdims=True) * (1.0 / hd)

    def norm_backward(tangent, unit, inv, gain_row):
        u = tangent * gain_row
        return (inv * (u - mean(u) - unit * mean(u * unit))).astype(BF16)

    def one_head(h, c):
        base = pl.multiple_of(h * 4 * length, tok)
        out_base = pl.multiple_of(h * 3 * length, tok)
        whole = in_buf.at[pl.ds(base, 4 * length)]
        pltpu.make_async_copy(whole, whole, in_recv.at[h]).wait()

        def norm(t, c):
            for a, held in ((0, q_aug), (1, k_aug)):
                rows = pl.ds(pl.multiple_of(t * RT, RT), RT)
                side_rows = pl.ds(pl.multiple_of(a * length + t * RT, RT), RT)
                x = in_buf[pl.ds(pl.multiple_of(base + a * length + t * RT, RT), RT), :].astype(F32)
                centered = x - mean(x)
                inv = lax.rsqrt(mean(centered * centered) + EPSILON)
                unit = centered * inv
                normed = unit * gains_ref[a : a + 1, :]
                held[rows, :hd] = normed.astype(BF16)
                unit_buf[side_rows, :] = unit
                inv_buf[side_rows, :] = jnp.broadcast_to(inv, (RT, hd))
                if a == 1:
                    k_turned[:, rows] = jnp.transpose(normed).astype(BF16)
                    dk_acc[rows, :] = jnp.zeros((RT, hd), F32)
                    dv_acc[rows, :] = jnp.zeros((RT, hd), F32)
            return c

        lax.fori_loop(0, length // RT, norm, 0)

        def panel(i, c):
            q_rows = pl.ds(pl.multiple_of(i * QT, QT), QT)
            q_tile = q_aug[q_rows, :]
            q_plain = q_aug[q_rows, :hd]
            g_tile = in_buf[pl.ds(pl.multiple_of(base + 3 * length + i * QT, QT), QT), :]
            first = jnp.maximum(i * QT - (MOST - 1), 0) // KT
            last = jnp.minimum(i * QT + QT - 1 + MOST - 1, length - 1) // KT + 1

            def chunk(j):
                return pl.ds(pl.multiple_of(j * KT, KT), KT)

            def scores(j, top):
                rows = chunk(j)
                s = contract_last(k_aug[rows, :], q_tile)
                s_buf[rows, :] = s
                v = in_buf[pl.ds(pl.multiple_of(base + 2 * length + j * KT, KT), KT), :]
                w_buf[rows, :] = contract_last(v, g_tile)
                return jnp.maximum(top, jnp.max(fold(s), axis=0))

            top = lax.fori_loop(first, last, scores, jnp.full((8, QT), -jnp.inf, F32))
            top = jnp.max(top, axis=0, keepdims=True)

            def exps(j, total):
                rows = chunk(j)
                e = jnp.exp2((s_buf[rows, :] - top) * exponent)
                s_buf[rows, :] = e
                return total + jnp.sum(fold(e), axis=0)

            total = lax.fori_loop(first, last, exps, jnp.zeros((8, QT), F32))
            over = 1.0 / jnp.sum(total, axis=0, keepdims=True)

            def weights(j, delta):
                rows = chunk(j)
                w = s_buf[rows, :] * over
                s_buf[rows, :] = w
                p = w.astype(BF16)
                p_buf[rows, :] = p
                return delta + jnp.sum(fold(p.astype(F32) * w_buf[rows, :]), axis=0)

            delta = lax.fori_loop(first, last, weights, jnp.zeros((8, QT), F32))
            delta = jnp.sum(delta, axis=0, keepdims=True)

            def grads(j, dq):
                rows = chunk(j)
                ds = (s_buf[rows, :] * (w_buf[rows, :] - delta)).astype(BF16)
                dv_acc[rows, :] += matmul(p_buf[rows, :], g_tile)
                dk_acc[rows, :] += matmul(ds, q_plain)
                return dq + matmul(k_turned[:, rows], ds)

            dq = lax.fori_loop(first, last, grads, jnp.zeros((hd, QT), F32))
            tangent = jnp.transpose(dq) * scaling
            unit = unit_buf[q_rows, :]
            out_rows = pl.ds(pl.multiple_of(out_base + i * QT, QT), QT)
            out_buf[out_rows, :] = norm_backward(
                tangent, unit, inv_buf[q_rows, :], gains_ref[0:1, :]
            )
            gain_acc[0:8, :] += jnp.sum(fold(tangent * unit), axis=0)
            return c

        lax.fori_loop(0, length // QT, panel, 0)

        def finish(t, c):
            rows = pl.ds(pl.multiple_of(t * RT, RT), RT)
            side_rows = pl.ds(pl.multiple_of(length + t * RT, RT), RT)
            tangent = dk_acc[rows, :] * scaling
            unit = unit_buf[side_rows, :]
            out_buf[pl.ds(pl.multiple_of(out_base + length + t * RT, RT), RT), :] = norm_backward(
                tangent, unit, inv_buf[side_rows, :], gains_ref[1:2, :]
            )
            gain_acc[8:16, :] += jnp.sum(fold(tangent * unit), axis=0)
            out_buf[pl.ds(pl.multiple_of(out_base + 2 * length + t * RT, RT), RT), :] = dv_acc[
                rows, :
            ].astype(BF16)
            return c

        lax.fori_loop(0, length // RT, finish, 0)

        @pl.when(h == heads - 1)
        def _():
            terms = [jnp.sum(gain_acc[8 * a : 8 * a + 8, :], axis=0, keepdims=True) for a in (0, 1)]
            own = jnp.concatenate(terms + [jnp.zeros((6, hd), F32)], axis=0)
            gain_acc[16:24, :] = own
            slot = pl.ds(pl.multiple_of(seq * 8, 8), 8)
            gain_seq[slot, :] = own

            def send_terms(i, c):
                remote(
                    gain_acc.at[pl.ds(16, 8)], gain_seq.at[slot],
                    gain_send.at[0], gain_recv.at[0], partner(i), mp,
                ).start()
                return c

            lax.fori_loop(1, n, send_terms, 0)

        targets = (oq_hbm, ok_hbm, ov_hbm)

        def out_rows(a, s):
            return pl.ds(pl.multiple_of(((h * 3 + a) * n + s) * tok, tok), tok)

        for a in range(3):
            pltpu.make_async_copy(
                out_buf.at[out_rows(a, seq)], targets[a].at[0, :, lanes(seq, h)], out_recv.at[0]
            ).start()

            def send_one(i, c, a=a):
                to = partner(i)
                remote(
                    out_buf.at[out_rows(a, to)], targets[a].at[0, :, lanes(seq, h)],
                    out_send.at[0], out_recv.at[0], to, mp,
                ).start()
                return c

            lax.fori_loop(1, n, send_one, 0)
        return c

    lax.fori_loop(0, heads, one_head, 0)

    got = gain_seq.at[pl.ds(0, (n - 1) * 8)]
    pltpu.make_async_copy(got, got, gain_recv.at[0]).wait()
    row_sum = jnp.sum(gain_seq[...].reshape(n, 8, hd), axis=0)
    gain_acc[24:32, :] = row_sum
    mp_slot = pl.ds(pl.multiple_of(mp * 8, 8), 8)
    gain_mp[mp_slot, :] = row_sum

    def send_sums(i, c):
        remote(
            gain_acc.at[pl.ds(24, 8)], gain_mp.at[mp_slot],
            gain_send.at[1], gain_recv.at[1], seq, mp_partner(i),
        ).start()
        return c

    lax.fori_loop(1, m, send_sums, 0)
    got = gain_mp.at[pl.ds(0, (m - 1) * 8)]
    pltpu.make_async_copy(got, got, gain_recv.at[1]).wait()
    total = jnp.sum(gain_mp[...].reshape(m, 8, hd), axis=0)
    gain_ref[...] = total[:2] * (length * n * heads) ** (-0.5)

    def drain(ref, sem):
        pltpu.make_async_copy(ref, ref, sem).wait()

    drain(id_buf.at[pl.ds(0, (n - 1) * 8)], id_send.at[0])
    drain(gain_seq.at[pl.ds(0, (n - 1) * 8)], gain_send.at[0])
    drain(gain_mp.at[pl.ds(0, (m - 1) * 8)], gain_send.at[1])
    drain(in_buf.at[pl.ds(0, heads * 4 * (n - 1) * tok)], in_send.at[0])
    drain(out_buf.at[pl.ds(0, heads * 3 * (n - 1) * tok)], out_send.at[0])
    drain(out_buf, out_recv.at[0])


def shards(n, m, query_raw, key_raw, value_rows, out_grads, image_ids, qk_gains):
    tok, width = query_raw.shape[1:]
    hd = qk_gains.shape[1]
    heads = width // hd // n
    length = n * tok
    grad = jax.ShapeDtypeStruct(query_raw.shape, BF16)
    hbm = pl.BlockSpec(memory_space=pl.ANY)
    vmem = pl.BlockSpec(memory_space=pltpu.VMEM)
    dma = pltpu.SemaphoreType.DMA
    return pl.pallas_call(
        functools.partial(kernel, n, m, heads, tok, hd),
        out_shape=(grad, grad, grad, jax.ShapeDtypeStruct((2, hd), F32)),
        in_specs=[hbm, hbm, hbm, hbm, vmem, vmem],
        out_specs=(hbm, hbm, hbm, vmem),
        scratch_shapes=[
            pltpu.VMEM((heads * 4 * length, hd), BF16),
            pltpu.VMEM((heads * 3 * length, hd), BF16),
            pltpu.VMEM((8, tok), jnp.int32),
            pltpu.VMEM((n * 8, tok), jnp.int32),
            pltpu.VMEM((length, 2 * hd), BF16),
            pltpu.VMEM((length, 2 * hd), BF16),
            pltpu.VMEM((hd, length), BF16),
            pltpu.VMEM((2 * length, hd), F32),
            pltpu.VMEM((2 * length, hd), F32),
            pltpu.VMEM((length, QT), F32),
            pltpu.VMEM((length, QT), F32),
            pltpu.VMEM((length, QT), BF16),
            pltpu.VMEM((length, hd), F32),
            pltpu.VMEM((length, hd), F32),
            pltpu.VMEM((32, hd), F32),
            pltpu.VMEM((n * 8, hd), F32),
            pltpu.VMEM((m * 8, hd), F32),
            dma((1,)), dma((heads,)), dma((1,)), dma((1,)), dma((1,)), dma((1,)), dma((2,)), dma((2,)),
        ],
        compiler_params=pltpu.CompilerParams(
            collective_id=0, has_side_effects=True, vmem_limit_bytes=56 * 2**20
        ),
    )(query_raw, key_raw, value_rows, out_grads, image_ids, qk_gains)


def solution(mesh):
    rows = P("mp", "seq", None)
    return jax.shard_map(
        functools.partial(shards, mesh.shape["seq"], mesh.shape["mp"]),
        mesh=mesh,
        in_specs=(rows, rows, rows, rows, P("mp", "seq"), P()),
        out_specs=(rows, rows, rows, P()),
        check_vma=False,
    )
```

time: 924 us -> 154 us (0.17); the launches traced: 912 us -> 153 us
  local copies, waits for them, and re-layouts: 309 us -> 6.49 us
  blocking collectives: 201 us -> 0 us
  other arithmetic: 192 us -> 0 us
  Pallas kernels: 0 us -> 146 us
  matrix products: 102 us -> 0 us
  waiting for transfers between devices: 41.5 us -> 0 us
  starting transfers between devices: 34.6 us -> 0 us
  loops' own time: 29.7 us -> 0 us
    psum x1 -> x0, blocking collectives: 171 us -> none  [shards(): lax.psum(gain_terms, ('seq', 'mp'))]
    pallas_call x0 -> x1, Pallas kernels: none -> 146 us  [shards(): pl.pallas_call(functools.partial(kernel, n, m, heads, tok, hd), out_shape...]
    another operation x58 -> x0, local copies, waits for them, and re-layouts: 108 us -> none
    dot_general x40 -> x0, matrix products: 86.8 us -> none  [the longest x8 23.3 us: compute_grads(): jnp.einsum('hqk,hkd->hqd', grad_scores, key_tile, preferred_element_type=...]
    convert_element_type x11 -> x0, other arithmetic: 62.1 us -> none  [the longest x4 41 us: block_step(): (attn_weights * (weight_grads - row_delta[:, :, None])).astype(jnp.bfloat16)]
    reduce_sum x19 -> x0, other arithmetic: 57.2 us -> none  [the longest x4 23.9 us: block_step(): attn_weights = exp_scores / jnp.sum(exp_scores, axis=2, keepdims=True)]
    cond x64 -> x0, local copies, waits for them, and re-layouts: 52.2 us -> none  [the longest x16 52.1 us: block_step(): score_list.append(lax.cond(live_row[j], compute_scores, empty_scores))]
    while x232 -> x0, local copies, waits for them, and re-layouts: 49.1 us -> none
  transfers between devices with their start and end apart: 7 -> 0, of which waited for: 5 -> 0; matrix products, arithmetic and copies ran while one was open for 8% -> 0% of each run, Pallas kernels for 0% -> 0%
where the time goes in v1:
time: 154 us; the launch traced here: 153 us
  Pallas kernels  146 us (95%)
  local copies, waits for them, and re-layouts  6.49 us (4%)
    pallas_call x1, Pallas kernels, shards(): pl.pallas_call(functools.partial(kernel, n, m, heads, tok, hd), out_shape...  146 us
    unnamed x10, local copies, waits for them, and re-layouts  6.49 us

profile of v1, /device:TPU:1, one launch (start us, length us, event | category | flops | bytes accessed | tf_op | source)
XLA Modules:
  0.0 153.4 jit_solution(8184377896727323078)
XLA Ops:
  0.6 146.3 %shard_map.93 = (bf16[1,128,6144]{2,1,0:T(8,128)(2,1)}, bf16[1,128,6144]{2,1,0:T(8,128)(2,1)}, bf16[1,128,6144]{2,1,0:T(8,128)(2,1)}, f32[2,128]{1,0:T(2,128)}) custom-call(bf16[1,128,6144]{2,1,0:T(8,128)(2,1)} %q_hbm.1, bf16[1,128,6144]{2,1,0:T(8,128)(2,1)} %k_hbm.1, bf16[1,128,6144]{2,1,0:T(8,128)(2,1)} %v_hbm.1, bf16[1,128,6144]{2,1,0:T(8,128)(2,1)} %g_hbm.1, ...), custom_call_target="tpu_custom_call" | custom-call | tf_op jit(solution)/shard_map/pallas_call | solution.py:320
  146.9 0.0 copy-start.1
  146.9 2.8 %copy.14 = bf16[1,128,6144]{2,1,0:T(8,128)(2,1)} copy(bf16[1,128,6144]{2,1,0:T(8,128)(2,1)} %get-tuple-element.8) | data formatting | bytes 3145728
  149.7 0.0 copy-done.1
  149.7 0.0 copy-start
  149.7 1.1 copy.15
  150.9 0.8 copy-done
  151.7 0.0 copy-start.2
  151.7 1.1 copy.16
  152.9 0.0 copy-done.2
  152.9 0.6 copy.17
Async XLA Ops:
  146.9 2.8 %copy-start.1 = (bf16[1,128,6144]{2,1,0:T(8,128)(2,1)S(1)}, bf16[1,128,6144]{2,1,0:T(8,128)(2,1)}, u32[]{:S(2)}) copy-start(bf16[1,128,6144]{2,1,0:T(8,128)(2,1)} %get-tuple-element.9) | copy-start | bytes 4718596
  149.7 2.0 %copy-start = (bf16[1,128,6144]{2,1,0:T(8,128)(2,1)S(1)}, bf16[1,128,6144]{2,1,0:T(8,128)(2,1)}, u32[]{:S(2)}) copy-start(bf16[1,128,6144]{2,1,0:T(8,128)(2,1)} %get-tuple-element.10) | copy-start | bytes 4718596
  151.7 1.1 copy-start.2

commit v2 on v1

--- a/solution.py
+++ b/solution.py
@@ -12,18 +12,14 @@
 EPSILON = 1e-06
 BAN = -32768.0
 CLASSES = 8
-QT = 256
+QT = 512
 KT = 512
-RT = 256
+RT = 1024
 MOST = 1024
 F32 = jnp.float32
 BF16 = jnp.bfloat16
 
 
-def contract_last(a, b):
-    return lax.dot_general(a, b, (((1,), (1,)), ((), ())), preferred_element_type=F32)
-
-
 def matmul(a, b):
     return lax.dot_general(a, b, (((1,), (0,)), ((), ())), preferred_element_type=F32)
 
@@ -34,11 +30,11 @@
 
 def kernel(
     n, m, heads, tok, hd,
-    q_hbm, k_hbm, v_hbm, g_hbm, ids_ref, gains_ref,
-    oq_hbm, ok_hbm, ov_hbm, gain_ref,
-    in_buf, out_buf, id_src, id_buf, q_aug, k_aug, k_turned, unit_buf, inv_buf,
+    q_hbm, k_hbm, v_hbm, g_hbm, ids_hbm, gains_hbm,
+    oq_ref, ok_ref, ov_ref, gain_ref,
+    in_buf, out_buf, ids_ref, gains_ref, id_src, id_buf, q_plain, q_turned, g_turned, k_aug, k_turned, unit_buf, inv_buf,
     s_buf, w_buf, p_buf, dk_acc, dv_acc, gain_acc, gain_seq, gain_mp,
-    in_send, in_recv, id_send, id_recv, out_send, out_recv, gain_send, gain_recv,
+    own_sems, in_send, in_recv, id_send, id_recv, out_send, out_recv, gain_send, gain_recv,
 ):
     seq, mp = lax.axis_index("seq"), lax.axis_index("mp")
     length = n * tok
@@ -47,6 +43,7 @@
     exponent = scaling * math.log2(math.e)
 
     def partner(i):
+        i = lax.rem(i * 7, n)
         z = lax.rem(seq // side + i // side, side)
         x = lax.rem(lax.rem(seq, side) + lax.rem(i, side), side)
         return z * side + x
@@ -60,6 +57,10 @@
             device_id=(to_seq, to_mp), device_id_type=MESH,
         )
 
+    own_ids = pltpu.make_async_copy(ids_hbm, ids_ref, own_sems.at[0])
+    own_gains = pltpu.make_async_copy(gains_hbm, gains_ref, own_sems.at[1])
+    own_ids.start()
+    own_gains.start()
     barrier = pltpu.get_barrier_semaphore()
 
     def greet_seq(i, c):
@@ -72,6 +73,8 @@
 
     lax.fori_loop(1, n, greet_seq, 0)
     lax.fori_loop(1, m, greet_mp, 0)
+    own_ids.wait()
+    own_gains.wait()
     id_src[...] = jnp.broadcast_to(ids_ref[...], (8, tok))
     id_buf[pl.ds(pl.multiple_of(seq * 8, 8), 8), :] = jnp.broadcast_to(ids_ref[...], (8, tok))
     pl.semaphore_wait(barrier, n - 1 + m - 1)
@@ -114,21 +117,23 @@
     ids_got = id_buf.at[pl.ds(0, (n - 1) * 8)]
     pltpu.make_async_copy(ids_got, ids_got, id_recv.at[0]).wait()
     lane = lax.broadcasted_iota(jnp.int32, (tok, hd), 1)
+    level = lax.broadcasted_iota(jnp.int32, (hd, tok), 0)
 
     def features(s, c):
         row = id_buf[pl.ds(pl.multiple_of(s * 8, 8), 8), :].astype(F32)[:1]
         image = jnp.transpose(jnp.broadcast_to(row, (hd, tok))).astype(jnp.int32)
-        same = image == lane
         rows = pl.ds(pl.multiple_of(s * tok, tok), tok)
-        q_aug[rows, hd:] = jnp.where(same, 1.0, 0.0).astype(BF16)
-        k_aug[rows, hd:] = jnp.where(jnp.logical_and(lane < CLASSES, ~same), BAN, 0.0).astype(BF16)
+        q_turned[hd:, rows] = jnp.where(row.astype(jnp.int32) == level, 1.0, 0.0).astype(BF16)
+        k_aug[rows, hd:] = jnp.where(
+            jnp.logical_and(lane < CLASSES, image != lane), BAN, 0.0
+        ).astype(BF16)
         return c
 
     lax.fori_loop(0, n, features, 0)
     gain_acc[...] = jnp.zeros_like(gain_acc)
 
     def mean(x):
-        return jnp.sum(x, axis=-1, keepdims=True) * (1.0 / hd)
+        return jnp.sum(x.astype(F32), axis=-1, keepdims=True) * (1.0 / hd)
 
     def norm_backward(tangent, unit, inv, gain_row):
         u = tangent * gain_row
@@ -141,29 +146,38 @@
         pltpu.make_async_copy(whole, whole, in_recv.at[h]).wait()
 
         def norm(t, c):
-            for a, held in ((0, q_aug), (1, k_aug)):
-                rows = pl.ds(pl.multiple_of(t * RT, RT), RT)
+            rows = pl.ds(pl.multiple_of(t * RT, RT), RT)
+
+            def arrived(a):
+                return in_buf[pl.ds(pl.multiple_of(base + a * length + t * RT, RT), RT), :]
+
+            for a in (0, 1):
                 side_rows = pl.ds(pl.multiple_of(a * length + t * RT, RT), RT)
-                x = in_buf[pl.ds(pl.multiple_of(base + a * length + t * RT, RT), RT), :].astype(F32)
-                centered = x - mean(x)
+                raw = arrived(a)
+                centered = raw.astype(F32) - mean(raw)
                 inv = lax.rsqrt(mean(centered * centered) + EPSILON)
                 unit = centered * inv
                 normed = unit * gains_ref[a : a + 1, :]
-                held[rows, :hd] = normed.astype(BF16)
                 unit_buf[side_rows, :] = unit
                 inv_buf[side_rows, :] = jnp.broadcast_to(inv, (RT, hd))
-                if a == 1:
+                if a == 0:
+                    q_plain[rows, :] = normed.astype(BF16)
+                    q_turned[:hd, rows] = jnp.transpose(normed).astype(BF16)
+                else:
+                    k_aug[rows, :hd] = normed.astype(BF16)
                     k_turned[:, rows] = jnp.transpose(normed).astype(BF16)
-                    dk_acc[rows, :] = jnp.zeros((RT, hd), F32)
-                    dv_acc[rows, :] = jnp.zeros((RT, hd), F32)
+            g_turned[:, rows] = jnp.transpose(arrived(3).astype(F32)).astype(BF16)
+            dk_acc[rows, :] = jnp.zeros((RT, hd), F32)
+            dv_acc[rows, :] = jnp.zeros((RT, hd), F32)
             return c
 
         lax.fori_loop(0, length // RT, norm, 0)
 
         def panel(i, c):
             q_rows = pl.ds(pl.multiple_of(i * QT, QT), QT)
-            q_tile = q_aug[q_rows, :]
-            q_plain = q_aug[q_rows, :hd]
+            q_tile = q_plain[q_rows, :]
+            q_turn = q_turned[:, q_rows]
+            g_turn = g_turned[:, q_rows]
             g_tile = in_buf[pl.ds(pl.multiple_of(base + 3 * length + i * QT, QT), QT), :]
             first = jnp.maximum(i * QT - (MOST - 1), 0) // KT
             last = jnp.minimum(i * QT + QT - 1 + MOST - 1, length - 1) // KT + 1
@@ -173,10 +187,10 @@
 
             def scores(j, top):
                 rows = chunk(j)
-                s = contract_last(k_aug[rows, :], q_tile)
+                s = matmul(k_aug[rows, :], q_turn)
                 s_buf[rows, :] = s
                 v = in_buf[pl.ds(pl.multiple_of(base + 2 * length + j * KT, KT), KT), :]
-                w_buf[rows, :] = contract_last(v, g_tile)
+                w_buf[rows, :] = matmul(v, g_turn)
                 return jnp.maximum(top, jnp.max(fold(s), axis=0))
 
             top = lax.fori_loop(first, last, scores, jnp.full((8, QT), -jnp.inf, F32))
@@ -206,7 +220,7 @@
                 rows = chunk(j)
                 ds = (s_buf[rows, :] * (w_buf[rows, :] - delta)).astype(BF16)
                 dv_acc[rows, :] += matmul(p_buf[rows, :], g_tile)
-                dk_acc[rows, :] += matmul(ds, q_plain)
+                dk_acc[rows, :] += matmul(ds, q_tile)
                 return dq + matmul(k_turned[:, rows], ds)
 
             dq = lax.fori_loop(first, last, grads, jnp.zeros((hd, QT), F32))
@@ -254,20 +268,20 @@
 
             lax.fori_loop(1, n, send_terms, 0)
 
-        targets = (oq_hbm, ok_hbm, ov_hbm)
+        targets = (oq_ref, ok_ref, ov_ref)
 
         def out_rows(a, s):
             return pl.ds(pl.multiple_of(((h * 3 + a) * n + s) * tok, tok), tok)
 
         for a in range(3):
             pltpu.make_async_copy(
-                out_buf.at[out_rows(a, seq)], targets[a].at[0, :, lanes(seq, h)], out_recv.at[0]
+                out_buf.at[out_rows(a, seq)], targets[a].at[:, lanes(seq, h)], out_recv.at[0]
             ).start()
 
             def send_one(i, c, a=a):
                 to = partner(i)
                 remote(
-                    out_buf.at[out_rows(a, to)], targets[a].at[0, :, lanes(seq, h)],
+                    out_buf.at[out_rows(a, to)], targets[a].at[:, lanes(seq, h)],
                     out_send.at[0], out_recv.at[0], to, mp,
                 ).start()
                 return c
@@ -308,26 +322,47 @@
     drain(out_buf, out_recv.at[0])
 
 
+def settle(q_ref, k_ref, v_ref, gain_in, oq_hbm, ok_hbm, ov_hbm, gain_hbm, sems):
+    parts = 4
+    rows = q_ref.shape[0] // parts
+    copies = [
+        pltpu.make_async_copy(a.at[piece], b.at[0, piece], sems.at[parts * i + p])
+        for i, (a, b) in enumerate(((q_ref, oq_hbm), (k_ref, ok_hbm), (v_ref, ov_hbm)))
+        for p, piece in enumerate(pl.ds(p * rows, rows) for p in range(parts))
+    ]
+    copies.append(pltpu.make_async_copy(gain_in, gain_hbm, sems.at[3 * parts]))
+    for copy in copies:
+        copy.start()
+    for copy in copies:
+        copy.wait()
+
+
 def shards(n, m, query_raw, key_raw, value_rows, out_grads, image_ids, qk_gains):
     tok, width = query_raw.shape[1:]
     hd = qk_gains.shape[1]
     heads = width // hd // n
     length = n * tok
+    landed = pltpu.VMEM((tok, width), BF16)
     grad = jax.ShapeDtypeStruct(query_raw.shape, BF16)
+    gain = jax.ShapeDtypeStruct((2, hd), F32)
     hbm = pl.BlockSpec(memory_space=pl.ANY)
     vmem = pl.BlockSpec(memory_space=pltpu.VMEM)
     dma = pltpu.SemaphoreType.DMA
-    return pl.pallas_call(
+    arrived = pl.pallas_call(
         functools.partial(kernel, n, m, heads, tok, hd),
-        out_shape=(grad, grad, grad, jax.ShapeDtypeStruct((2, hd), F32)),
-        in_specs=[hbm, hbm, hbm, hbm, vmem, vmem],
-        out_specs=(hbm, hbm, hbm, vmem),
+        out_shape=(landed, landed, landed, pltpu.VMEM((2, hd), F32)),
+        in_specs=[hbm, hbm, hbm, hbm, hbm, hbm],
+        out_specs=(vmem, vmem, vmem, vmem),
         scratch_shapes=[
             pltpu.VMEM((heads * 4 * length, hd), BF16),
             pltpu.VMEM((heads * 3 * length, hd), BF16),
+            pltpu.VMEM((1, tok), jnp.int32),
+            pltpu.VMEM((2, hd), F32),
             pltpu.VMEM((8, tok), jnp.int32),
             pltpu.VMEM((n * 8, tok), jnp.int32),
-            pltpu.VMEM((length, 2 * hd), BF16),
+            pltpu.VMEM((length, hd), BF16),
+            pltpu.VMEM((2 * hd, length), BF16),
+            pltpu.VMEM((hd, length), BF16),
             pltpu.VMEM((length, 2 * hd), BF16),
             pltpu.VMEM((hd, length), BF16),
             pltpu.VMEM((2 * length, hd), F32),
@@ -340,12 +375,24 @@
             pltpu.VMEM((32, hd), F32),
             pltpu.VMEM((n * 8, hd), F32),
             pltpu.VMEM((m * 8, hd), F32),
-            dma((1,)), dma((heads,)), dma((1,)), dma((1,)), dma((1,)), dma((1,)), dma((2,)), dma((2,)),
+            dma((2,)), dma((1,)), dma((heads,)), dma((1,)), dma((1,)), dma((1,)), dma((1,)), dma((2,)), dma((2,)),
         ],
         compiler_params=pltpu.CompilerParams(
-            collective_id=0, has_side_effects=True, vmem_limit_bytes=56 * 2**20
+            collective_id=0, has_side_effects=True, vmem_limit_bytes=48 * 2**20
         ),
-    )(query_raw, key_raw, value_rows, out_grads, image_ids, qk_gains)
+    )(
+        query_raw, key_raw, value_rows, out_grads,
+        pltpu.with_memory_space_constraint(image_ids, pltpu.HBM),
+        pltpu.with_memory_space_constraint(qk_gains, pltpu.HBM),
+    )
+    return pl.pallas_call(
+        settle,
+        out_shape=(grad, grad, grad, gain),
+        in_specs=[vmem, vmem, vmem, vmem],
+        out_specs=(hbm, hbm, hbm, hbm),
+        scratch_shapes=[dma((13,))],
+        compiler_params=pltpu.CompilerParams(vmem_limit_bytes=2**20),
+    )(*(pltpu.with_memory_space_constraint(a, pltpu.VMEM) for a in arrived))
 
 
 def solution(mesh):

time: 154 us -> 134 us (0.87)
  Pallas kernels: 146 us -> 133 us
  local copies, waits for them, and re-layouts: 6.49 us -> 0 us
    pallas_call x1, Pallas kernels: 146 us -> 130 us  [shards(): pl.pallas_call(functools.partial(kernel, n, m, heads, tok, hd), out_shape...]
    unnamed x10 -> x0, local copies, waits for them, and re-layouts: 6.49 us -> none
    pallas_call x0 -> x1, Pallas kernels: none -> 2.29 us  [shards(): pl.pallas_call(settle, out_shape=(grad, grad, grad, gain), in_specs=[vmem...]
where the time goes in v2:
time: 134 us; the launch traced here: 133 us
  Pallas kernels  133 us (99%)
    pallas_call x1, Pallas kernels, shards(): pl.pallas_call(functools.partial(kernel, n, m, heads, tok, hd), out_shape...  130 us

profile of v2, /device:TPU:1, one launch (start us, length us, event | category | flops | bytes accessed | tf_op | source)
XLA Modules:
  0.0 133.4 jit_solution(16829128829151598242)
XLA Ops:
  0.6 130.5 %shard_map.93 = (bf16[128,6144]{1,0:T(8,128)(2,1)S(1)}, bf16[128,6144]{1,0:T(8,128)(2,1)S(1)}, bf16[128,6144]{1,0:T(8,128)(2,1)S(1)}, f32[2,128]{1,0:T(2,128)S(1)}) custom-call(bf16[1,128,6144]{2,1,0:T(8,128)(2,1)} %q_hbm.1, bf16[1,128,6144]{2,1,0:T(8,128)(2,1)} %k_hbm.1, bf16[1,128,6144]{2,1,0:T(8,128)(2,1)} %v_hbm.1, bf16[1,128,6144]{2,1,0:T(8,128)(2,1)} %g_hbm.1, ...), custom_call_target="tpu_custom_call" | custom-call | tf_op jit(solution)/shard_map/pallas_call | solution.py:351
  131.1 2.3 %shard_map.94 = (bf16[1,128,6144]{2,1,0:T(8,128)(2,1)}, bf16[1,128,6144]{2,1,0:T(8,128)(2,1)}, bf16[1,128,6144]{2,1,0:T(8,128)(2,1)}, f32[2,128]{1,0:T(2,128)}) custom-call(bf16[128,6144]{1,0:T(8,128)(2,1)S(1)} %get-tuple-element.8.q_ref, bf16[128,6144]{1,0:T(8,128)(2,1)S(1)} %get-tuple-element.9.k_ref, bf16[128,6144]{1,0:T(8,128)(2,1)S(1)} %get-tuple-element.10.v_ref, ...), custom_call_target="tpu_custom_call" | custom-call | tf_op jit(solution)/shard_map/pallas_call | solution.py:388

commit v3 on v2

--- a/solution.py
+++ b/solution.py
@@ -13,8 +13,8 @@
 BAN = -32768.0
 CLASSES = 8
 QT = 512
-KT = 512
-RT = 1024
+KT = 2048
+RT = 2048
 MOST = 1024
 F32 = jnp.float32
 BF16 = jnp.bfloat16
@@ -33,7 +33,7 @@
     q_hbm, k_hbm, v_hbm, g_hbm, ids_hbm, gains_hbm,
     oq_ref, ok_ref, ov_ref, gain_ref,
     in_buf, out_buf, ids_ref, gains_ref, id_src, id_buf, q_plain, q_turned, g_turned, k_aug, k_turned, unit_buf, inv_buf,
-    s_buf, w_buf, p_buf, dk_acc, dv_acc, gain_acc, gain_seq, gain_mp,
+    s_buf, w_buf, dk_acc, dv_acc, gain_acc, gain_seq, gain_mp,
     own_sems, in_send, in_recv, id_send, id_recv, out_send, out_recv, gain_send, gain_recv,
 ):
     seq, mp = lax.axis_index("seq"), lax.axis_index("mp")
@@ -189,15 +189,15 @@
                 rows = chunk(j)
                 s = matmul(k_aug[rows, :], q_turn)
                 s_buf[rows, :] = s
+                return jnp.maximum(top, jnp.max(fold(s), axis=0))
+
+            top = lax.fori_loop(first, last, scores, jnp.full((8, QT), -jnp.inf, F32))
+            top = jnp.max(top, axis=0, keepdims=True)
+
+            def exps(j, total):
+                rows = chunk(j)
                 v = in_buf[pl.ds(pl.multiple_of(base + 2 * length + j * KT, KT), KT), :]
                 w_buf[rows, :] = matmul(v, g_turn)
-                return jnp.maximum(top, jnp.max(fold(s), axis=0))
-
-            top = lax.fori_loop(first, last, scores, jnp.full((8, QT), -jnp.inf, F32))
-            top = jnp.max(top, axis=0, keepdims=True)
-
-            def exps(j, total):
-                rows = chunk(j)
                 e = jnp.exp2((s_buf[rows, :] - top) * exponent)
                 s_buf[rows, :] = e
                 return total + jnp.sum(fold(e), axis=0)
@@ -210,7 +210,7 @@
                 w = s_buf[rows, :] * over
                 s_buf[rows, :] = w
                 p = w.astype(BF16)
-                p_buf[rows, :] = p
+                dv_acc[rows, :] += matmul(p, g_tile)
                 return delta + jnp.sum(fold(p.astype(F32) * w_buf[rows, :]), axis=0)
 
             delta = lax.fori_loop(first, last, weights, jnp.zeros((8, QT), F32))
@@ -219,7 +219,6 @@
             def grads(j, dq):
                 rows = chunk(j)
                 ds = (s_buf[rows, :] * (w_buf[rows, :] - delta)).astype(BF16)
-                dv_acc[rows, :] += matmul(p_buf[rows, :], g_tile)
                 dk_acc[rows, :] += matmul(ds, q_tile)
                 return dq + matmul(k_turned[:, rows], ds)
 
@@ -323,7 +322,7 @@
 
 
 def settle(q_ref, k_ref, v_ref, gain_in, oq_hbm, ok_hbm, ov_hbm, gain_hbm, sems):
-    parts = 4
+    parts = 2
     rows = q_ref.shape[0] // parts
     copies = [
         pltpu.make_async_copy(a.at[piece], b.at[0, piece], sems.at[parts * i + p])
@@ -369,7 +368,6 @@
             pltpu.VMEM((2 * length, hd), F32),
             pltpu.VMEM((length, QT), F32),
             pltpu.VMEM((length, QT), F32),
-            pltpu.VMEM((length, QT), BF16),
             pltpu.VMEM((length, hd), F32),
             pltpu.VMEM((length, hd), F32),
             pltpu.VMEM((32, hd), F32),
@@ -390,7 +388,7 @@
         out_shape=(grad, grad, grad, gain),
         in_specs=[vmem, vmem, vmem, vmem],
         out_specs=(hbm, hbm, hbm, hbm),
-        scratch_shapes=[dma((13,))],
+        scratch_shapes=[dma((7,))],
         compiler_params=pltpu.CompilerParams(vmem_limit_bytes=2**20),
     )(*(pltpu.with_memory_space_constraint(a, pltpu.VMEM) for a in arrived))
 

time: 134 us -> 133 us (level)
  no operation moved by 1% of the time
where the time goes in v3:
time: 133 us
  Pallas kernels  133 us (100%)
    pallas_call x1, Pallas kernels, shards(): pl.pallas_call(functools.partial(kernel, n, m, heads, tok, hd), out_shape...  130 us

profile of v3, /device:TPU:1, one launch (start us, length us, event | category | flops | bytes accessed | tf_op | source)
XLA Modules:
  0.0 133.4 jit_solution(14764296394589321927)
XLA Ops:
  0.6 130.5 %shard_map.93 = (bf16[128,6144]{1,0:T(8,128)(2,1)S(1)}, bf16[128,6144]{1,0:T(8,128)(2,1)S(1)}, bf16[128,6144]{1,0:T(8,128)(2,1)S(1)}, f32[2,128]{1,0:T(2,128)S(1)}) custom-call(bf16[1,128,6144]{2,1,0:T(8,128)(2,1)} %q_hbm.1, bf16[1,128,6144]{2,1,0:T(8,128)(2,1)} %k_hbm.1, bf16[1,128,6144]{2,1,0:T(8,128)(2,1)} %v_hbm.1, bf16[1,128,6144]{2,1,0:T(8,128)(2,1)} %g_hbm.1, ...), custom_call_target="tpu_custom_call" | custom-call | tf_op jit(solution)/shard_map/pallas_call | solution.py:350
  131.1 2.2 %shard_map.94 = (bf16[1,128,6144]{2,1,0:T(8,128)(2,1)}, bf16[1,128,6144]{2,1,0:T(8,128)(2,1)}, bf16[1,128,6144]{2,1,0:T(8,128)(2,1)}, f32[2,128]{1,0:T(2,128)}) custom-call(bf16[128,6144]{1,0:T(8,128)(2,1)S(1)} %get-tuple-element.8.q_ref, bf16[128,6144]{1,0:T(8,128)(2,1)S(1)} %get-tuple-element.9.k_ref, bf16[128,6144]{1,0:T(8,128)(2,1)S(1)} %get-tuple-element.10.v_ref, ...), custom_call_target="tpu_custom_call" | custom-call | tf_op jit(solution)/shard_map/pallas_call | solution.py:386
